TPU v7x, 32 devices: a whole 2x2x4 slice. The times are simulated.
32 devices in a mesh: dp: 8 (over z, y), rows: 4 (over x, core).
Axes of the slice: x: 2, y: 2, z: 4, core: 2. Of those that a mesh axis runs over, the one named last changes fastest.
Arguments:
- images: bfloat16 [8, 48, 64, 256], P('dp', 'rows'), may hold values from -6 to 6
- kernel: bfloat16 [3, 3, 256, 256], replicated, may hold values from -0.125 to 0.125
- cotangent: bfloat16 [8, 48, 64, 256], P('dp', 'rows'), may hold values from -6 to 6
Outputs:
- output_maps: bfloat16 [8, 48, 64, 256], P('dp', 'rows')
- grad_input: bfloat16 [8, 48, 64, 256], P('dp', 'rows')
- grad_kernel: float32 [3, 3, 256, 256], P(None, None, None, 'rows')
All inputs are finite; a program needn't handle non-finite values.
Results may differ from a plain program's by a relative error of at most 0.001.
Values may be sent and summed in bfloat16 or wider, within the bound.
A program may use at most 64 MiB of HBM per device.

v0:
```python
import jax
import jax.numpy as jnp
from jax import lax
from jax.sharding import PartitionSpec as P


def padded_2(x, sides, width):
    for axis, dim in sides:
        size, length = (lax.axis_size(axis), x.shape[dim])
        up = [(i, (i + 1) % size) for i in range(size - 1)]
        down = [(j, i) for i, j in up]
        last = lax.slice_in_dim(x, length - width, length, axis=dim)
        initial = lax.slice_in_dim(x, 0, width, axis=dim)
        before = lax.ppermute(last, axis, up)
        after = lax.ppermute(initial, axis, down)
        x = jnp.concatenate([before, x, after], axis=dim)
    return x


def conv_rows(inputs, weights):
    return lax.conv_general_dilated(
        inputs,
        weights,
        (1, 1),
        ((0, 0), (1, 1)),
        dimension_numbers=("NHWC", "HWIO", "NHWC"),
        preferred_element_type=jnp.float32,
    )


def shards(images, kernel, cotangent):
    rows_dev = images.shape[1]
    columns = images.shape[2]
    wide_images = padded_2(images, (("rows", 1),), 1)
    wide_grads = padded_2(cotangent, (("rows", 1),), 1)
    flipped = jnp.transpose(kernel[::-1, ::-1], (0, 1, 3, 2))
    output_maps = conv_rows(wide_images, kernel).astype(jnp.bfloat16)
    grad_input = conv_rows(wide_grads, flipped).astype(jnp.bfloat16)
    padded = jnp.pad(wide_images, ((0, 0), (0, 0), (1, 1), (0, 0)))
    tap_rows = []
    for tap_row in range(3):
        tap_line = []
        for tap_col in range(3):
            window = padded[:, tap_row : tap_row + rows_dev, tap_col : tap_col + columns]
            tap_line.append(
                jnp.einsum("bhwc,bhwd->cd", window, cotangent, preferred_element_type=jnp.float32)
            )
        tap_rows.append(jnp.stack(tap_line))
    local_terms = jnp.stack(tap_rows)
    groups = lax.axis_size("dp")
    row_share = lax.psum_scatter(local_terms, "rows", scatter_dimension=3, tiled=True)
    summed = lax.psum(row_share, "dp")
    batch_total = images.shape[0] * groups
    return (output_maps, grad_input, summed / float(batch_total))


def solution(mesh):
    return jax.shard_map(
        shards,
        mesh=mesh,
        in_specs=(P("dp", "rows", None, None), P(), P("dp", "rows", None, None)),
        out_specs=(
            P("dp", "rows", None, None),
            P("dp", "rows", None, None),
            P(None, None, None, "rows"),
        ),
        check_vma=False,
    )
```

profile of v0, /device:TPU:0, one launch (start us, length us, event | category | flops | bytes accessed | tf_op | source)
XLA Modules:
  0.0 180.4 jit_solution(7106152800115837669)
XLA Ops:
  7.2 0.0 copy-start
  7.2 0.0 copy-start.3
  7.2 0.0 copy-start.1
  7.2 0.0 all-reduce.7.cloned.1.call-start
  7.2 0.9 fusion.67
  8.2 2.3 %collective-permute-start = (bf16[1,1,64,256]{3,2,1,0:T(8,128)(2,1)S(1)}, bf16[1,1,64,256]{3,2,1,0:T(8,128)(2,1)S(1)}, u32[]{:S(2)}, u32[]{:S(2)}) collective-permute-start(bf16[1,1,64,256]{3,2,1,0:T(8,128)(2,1)S(1)} %get-tuple-element.15), channel_id=1, source_target_pairs={{0,1},{1,2},{2,3},{4,5},{5,6},{6,7},{8,9},{9,10},{10,11},{12,13},{... | collective-permute-start | bytes 98312 | tf_op jit(solution)/shard_map/ppermute | solution.py:14
  10.5 1.3 collective-permute-start.1
  11.8 1.4 convolution_bitcast_fusion.4
  13.3 2.4 %collective-permute-done.1 = bf16[1,1,64,256]{3,2,1,0:T(8,128)(2,1)S(1)} collective-permute-done((bf16[1,1,64,256]{3,2,1,0:T(8,128)(2,1)S(1)}, bf16[1,1,64,256]{3,2,1,0:T(8,128)(2,1)S(1)}, u32[]{:S(2)}, u32[]{:S(2)}) %collective-permute-start.1) | collective-permute-done | bytes 32800 | tf_op jit(solution)/shard_map/ppermute | solution.py:15
  15.7 0.3 convolution_bitcast_fusion.3
  16.0 0.3 convolution_bitcast_fusion.5
  16.4 0.3 convolution_bitcast_fusion.6
  16.7 0.3 convolution_bitcast_fusion.8
  17.0 0.3 convolution_bitcast_fusion
  17.3 0.3 convolution_bitcast_fusion.2
  17.6 0.3 convolution_bitcast_fusion.1
  17.9 0.1 maximum_bitcast_fusion.2
  18.0 0.3 convolution_bitcast_fusion.7
  18.3 0.1 maximum_bitcast_fusion
  18.4 0.2 pad_maximum_fusion
  18.6 2.9 %copy.26 = f32[3,3,256,256]{2,1,0,3:T(4,128)} copy(f32[3,3,256,256]{3,2,1,0:T(8,128)S(1)} %pad_maximum_fusion) | data formatting | bytes 4718592 | tf_op jit(solution)/shard_map/stack | solution.py:49
  21.5 0.0 all-reduce.7.cloned.1.call-update
  21.5 0.0 all-reduce.5.cloned.1.call-start
  21.6 0.9 copy-done.2
  22.5 4.5 %collective-permute-start.2 = (bf16[1,1,64,256]{3,2,1,0:T(8,128)(2,1)S(1)}, bf16[1,1,64,256]{3,2,1,0:T(8,128)(2,1)S(1)}, u32[]{:S(2)}, u32[]{:S(2)}) collective-permute-start(bf16[1,1,64,256]{3,2,1,0:T(8,128)(2,1)S(1)} %get-tuple-element.12), channel_id=1, source_target_pairs={{0,1},{1,2},{2,3},{4,5},{5,6},{6,7},{8,9},{9,10},{10,11},{12,13},{... | collective-permute-start | bytes 98312 | tf_op jit(solution)/shard_map/ppermute | solution.py:14
  27.0 1.3 collective-permute-start.3
  28.3 0.6 dynamic-slice
  29.6 0.3 copy.30
  29.9 0.0 copy-start.7
  29.9 0.1 pad.5.clone
  29.9 0.2 copy.20
  30.1 0.4 copy-done.7
  30.6 1.2 fusion
  31.8 0.1 copy.21
  31.9 61.2 %all-reduce.7.cloned.1.call-done = f32[3,3,256,256]{2,1,0,3:T(4,128)} async-done(((f32[3,3,256,256]{2,1,0,3:T(4,128)}), f32[3,3,256,256]{2,1,0,3:T(4,128)}) %all-reduce.7.cloned.1.call-update) | async-done | bytes 2359312
  93.1 2.2 %constant_dynamic-slice_fusion = f32[3,3,256,64]{2,1,0,3:T(4,128)} fusion(f32[3,3,256,256]{2,1,0,3:T(4,128)} %all-reduce.7.cloned.1.call-done, u32[]{:T(128)S(6)} %multiply.2), kind=kLoop, calls=%fused_computation.73 | loop fusion | bytes 1179652
  95.2 0.0 all-reduce.5.cloned.1.call-update
  95.3 0.1 maximum_bitcast_fusion.3
  95.4 0.9 copy.27
  96.2 0.3 copy.31
  96.5 0.1 pad.7.clone
  96.5 0.2 copy.24
  96.8 1.2 fusion.1
  98.0 0.1 copy.25
  98.2 0.9 copy.28
  99.0 72.3 %all-reduce.5.cloned.1.call-done = f32[3,3,256,64]{2,1,0,3:T(4,128)} async-done(((f32[3,3,256,64]{2,1,0,3:T(4,128)}), f32[3,3,256,64]{2,1,0,3:T(4,128)}) %all-reduce.5.cloned.1.call-update) | async-done | bytes 589840 | tf_op jit(solution)/shard_map/psum | solution.py:52
  171.3 1.3 broadcast_multiply_fusion
  172.6 0.9 copy.29
  (21 shorter events, 0.2 us)
Async XLA Ops:
  7.2 23.0 %copy-start = (bf16[3,3,256,256]{3,2,1,0:T(8,128)(2,1)S(1)}, bf16[3,3,256,256]{3,2,1,0:T(8,128)(2,1)}, u32[]{:S(2)}) copy-start(bf16[3,3,256,256]{3,2,1,0:T(8,128)(2,1)} %param.4) | copy-start | bytes 3538948
  7.2 6.1 %copy-start.3 = (bf16[1,12,64,256]{3,2,1,0:T(8,128)(2,1)S(1)}, bf16[1,12,64,256]{3,2,1,0:T(8,128)(2,1)}, u32[]{:S(2)}) copy-start(bf16[1,12,64,256]{3,2,1,0:T(8,128)(2,1)} %param.3) | copy-start | bytes 1179652
  7.2 8.5 %copy-start.1 = (bf16[1,12,64,256]{3,2,1,0:T(8,128)(2,1)S(1)}, bf16[1,12,64,256]{3,2,1,0:T(8,128)(2,1)}, u32[]{:S(2)}) copy-start(bf16[1,12,64,256]{3,2,1,0:T(8,128)(2,1)} %param.5) | copy-start | bytes 1179652
  7.2 85.9 %all-reduce.7.cloned.1.call-start = ((), (), s32[]{:S(2)}) async-start(), calls=%async_computation.1 | async-start | bytes 6291456
  8.2 5.1 %collective-permute-start = (bf16[1,1,64,256]{3,2,1,0:T(8,128)(2,1)S(1)}, bf16[1,1,64,256]{3,2,1,0:T(8,128)(2,1)S(1)}, u32[]{:S(2)}, u32[]{:S(2)}) collective-permute-start(bf16[1,1,64,256]{3,2,1,0:T(8,128)(2,1)S(1)} %get-tuple-element.15), channel_id=1, source_target_pairs={{0,1},{1,2},{2,3},{4,5},{5,6},{6,7},{8,9},{9,10},{10,11},{12,13},{... | collective-permute-start | bytes 98312 | tf_op jit(solution)/shard_map/ppermute | solution.py:14
  10.5 5.2 %collective-permute-start.1 = (bf16[1,1,64,256]{3,2,1,0:T(8,128)(2,1)S(1)}, bf16[1,1,64,256]{3,2,1,0:T(8,128)(2,1)S(1)}, u32[]{:S(2)}, u32[]{:S(2)}) collective-permute-start(bf16[1,1,64,256]{3,2,1,0:T(8,128)(2,1)S(1)} %get-tuple-element.14), channel_id=1, source_target_pairs={{1,0},{2,1},{3,2},{5,4},{6,5},{7,6},{9,8},{10,9},{11,10},{13,12},{... | collective-permute-start | bytes 98312 | tf_op jit(solution)/shard_map/ppermute | solution.py:15
  15.7 1.6 copy-start.4
  21.5 1.0 copy-start.2
  21.5 6.8 %copy-start.6 = (u32[32]{0:T(128)S(1)}, u32[32]{0:T(128)}, u32[]{:S(2)}) copy-start(u32[32]{0:T(128)} %constant.22) | copy-start | bytes 388
  21.5 8.1 %copy-start.5 = (bf16[1,14,64,256]{3,2,1,0:T(8,128)(2,1)S(1)}, bf16[1,14,64,256]{3,2,1,0:T(8,128)(2,1)}, u32[]{:S(2)}) copy-start(bf16[1,14,64,256]{3,2,1,0:T(8,128)(2,1)} %copy-done.4) | copy-start | bytes 1376260
  21.5 149.8 %all-reduce.5.cloned.1.call-start = ((), (), s32[]{:S(2)}) async-start(), calls=%async_computation | async-start | bytes 1572864 | tf_op jit(solution)/shard_map/psum | solution.py:52
  22.5 72.8 %collective-permute-start.2 = (bf16[1,1,64,256]{3,2,1,0:T(8,128)(2,1)S(1)}, bf16[1,1,64,256]{3,2,1,0:T(8,128)(2,1)S(1)}, u32[]{:S(2)}, u32[]{:S(2)}) collective-permute-start(bf16[1,1,64,256]{3,2,1,0:T(8,128)(2,1)S(1)} %get-tuple-element.12), channel_id=1, source_target_pairs={{0,1},{1,2},{2,3},{4,5},{5,6},{6,7},{8,9},{9,10},{10,11},{12,13},{... | collective-permute-start | bytes 98312 | tf_op jit(solution)/shard_map/ppermute | solution.py:14
  27.0 68.3 %collective-permute-start.3 = (bf16[1,1,64,256]{3,2,1,0:T(8,128)(2,1)S(1)}, bf16[1,1,64,256]{3,2,1,0:T(8,128)(2,1)S(1)}, u32[]{:S(2)}, u32[]{:S(2)}) collective-permute-start(bf16[1,1,64,256]{3,2,1,0:T(8,128)(2,1)S(1)} %get-tuple-element.13), channel_id=1, source_target_pairs={{1,0},{2,1},{3,2},{5,4},{6,5},{7,6},{9,8},{10,9},{11,10},{13,12},{... | collective-permute-start | bytes 98312 | tf_op jit(solution)/shard_map/ppermute | solution.py:15
  29.9 0.7 copy-start.7
Sparse Core Ops, SparseCore 0:
  21.6 71.3 all-reduce.6
  96.5 74.8 all-reduce.4
where the time goes:
time: 181 us; the launch traced here: 180 us
  waiting for transfers between devices  136 us (75%)
  between operations  15 us (8%)
  local copies, waits for them, and re-layouts  11.9 us (7%)
  starting transfers between devices  9.53 us (5%)
  matrix products  6.31 us (3%)
    psum x1, waiting for transfers between devices, shards(): summed = lax.psum(row_share, 'dp')  72.3 us
    unnamed x3, waiting for transfers between devices  61.2 us
    unnamed x25, local copies, waits for them, and re-layouts  7.31 us
    ppermute x2, starting transfers between devices, padded_2(): before = lax.ppermute(last, axis, up)  6.87 us
    dot_general x9, matrix products, shards(): jnp.einsum('bhwc,bhwd->cd', window, cotangent, preferred_element_type=jnp...  3.87 us
  transfers between devices with their start and end apart: 6, of which 3 were waited for; matrix products, arithmetic and copies ran while one was open for 5% of the time, Pallas kernels for 0%

commit v1 on v0

--- a/solution.py
+++ b/solution.py
@@ -49,7 +49,9 @@
     local_terms = jnp.stack(tap_rows)
     groups = lax.axis_size("dp")
     row_share = lax.psum_scatter(local_terms, "rows", scatter_dimension=3, tiled=True)
-    summed = lax.psum(row_share, "dp")
+    summed = row_share
+    for hop in (1, 2, 4):
+        summed = summed + lax.ppermute(summed, "dp", [(dev, dev ^ hop) for dev in range(8)])
     batch_total = images.shape[0] * groups
     return (output_maps, grad_input, summed / float(batch_total))
 

time: 181 us -> 158 us (0.87)
  waiting for transfers between devices: 136 us -> 113 us
  starting transfers between devices: 9.53 us -> 11.8 us
  local copies, waits for them, and re-layouts: 11.9 us -> 9.9 us
    psum x1 -> x0, waiting for transfers between devices: 72.3 us -> none  [shards(): summed = lax.psum(row_share, 'dp')]
    ppermute x0 -> x3, waiting for transfers between devices: none -> 41.7 us  [shards(): lax.ppermute(summed, 'dp', [(dev, dev ^ hop) for dev in range(8)])]
    unnamed x3 -> x2, waiting for transfers between devices: 61.2 us -> 69.3 us
    ppermute x0 -> x3, starting transfers between devices: none -> 5.56 us  [shards(): lax.ppermute(summed, 'dp', [(dev, dev ^ hop) for dev in range(8)])]
    ppermute x2, starting transfers between devices: 6.87 us -> 3.64 us  [padded_2(): before = lax.ppermute(last, axis, up)]
    unnamed x25 -> x24, local copies, waits for them, and re-layouts: 7.31 us -> 5.2 us
  transfers between devices with their start and end apart: 6 -> 8, of which waited for: 3 -> 5; matrix products, arithmetic and copies ran while one was open for 5% -> 5% of each run, Pallas kernels for 0% -> 0%
where the time goes in v1:
time: 158 us
  waiting for transfers between devices  113 us (72%)
  between operations  15 us (9%)
  starting transfers between devices  11.8 us (7%)
  local copies, waits for them, and re-layouts  9.9 us (6%)
  matrix products  6.31 us (4%)
    unnamed x2, waiting for transfers between devices  69.3 us
    ppermute x3, waiting for transfers between devices, shards(): lax.ppermute(summed, 'dp', [(dev, dev ^ hop) for dev in range(8)])  41.7 us
    ppermute x3, starting transfers between devices, shards(): lax.ppermute(summed, 'dp', [(dev, dev ^ hop) for dev in range(8)])  5.56 us
    unnamed x24, local copies, waits for them, and re-layouts  5.2 us
    dot_general x9, matrix products, shards(): jnp.einsum('bhwc,bhwd->cd', window, cotangent, preferred_element_type=jnp...  3.87 us
    ppermute x2, starting transfers between devices, padded_2(): before = lax.ppermute(last, axis, up)  3.64 us
  transfers between devices with their start and end apart: 8, of which 5 were waited for; matrix products, arithmetic and copies ran while one was open for 5% of the time, Pallas kernels for 0%

profile of v1, /device:TPU:0, one launch (start us, length us, event | category | flops | bytes accessed | tf_op | source)
XLA Modules:
  0.0 158.0 jit_solution(16389704860598635064)
XLA Ops:
  7.2 0.0 all-reduce.4.cloned.1.call-start
  7.2 0.9 fusion.67
  8.2 2.3 %collective-permute-start = (bf16[1,1,64,256]{3,2,1,0:T(8,128)(2,1)S(1)}, bf16[1,1,64,256]{3,2,1,0:T(8,128)(2,1)S(1)}, u32[]{:S(2)}, u32[]{:S(2)}) collective-permute-start(bf16[1,1,64,256]{3,2,1,0:T(8,128)(2,1)S(1)} %get-tuple-element.18), channel_id=1, source_target_pairs={{0,1},{1,2},{2,3},{4,5},{5,6},{6,7},{8,9},{9,10},{10,11},{12,13},{... | collective-permute-start | bytes 98312 | tf_op jit(solution)/shard_map/ppermute | solution.py:14
  10.5 1.3 collective-permute-start.1
  11.8 1.4 convolution_bitcast_fusion.4
  13.3 2.4 %collective-permute-done.1 = bf16[1,1,64,256]{3,2,1,0:T(8,128)(2,1)S(1)} collective-permute-done((bf16[1,1,64,256]{3,2,1,0:T(8,128)(2,1)S(1)}, bf16[1,1,64,256]{3,2,1,0:T(8,128)(2,1)S(1)}, u32[]{:S(2)}, u32[]{:S(2)}) %collective-permute-start.1) | collective-permute-done | bytes 32800 | tf_op jit(solution)/shard_map/ppermute | solution.py:15
  15.7 0.3 convolution_bitcast_fusion.3
  16.0 0.3 convolution_bitcast_fusion.5
  16.4 0.3 convolution_bitcast_fusion.6
  16.7 0.3 convolution_bitcast_fusion.8
  17.0 0.3 convolution_bitcast_fusion
  17.3 0.3 convolution_bitcast_fusion.2
  17.6 0.3 convolution_bitcast_fusion.1
  17.9 0.1 maximum_bitcast_fusion.2
  18.0 0.3 convolution_bitcast_fusion.7
  18.3 0.1 maximum_bitcast_fusion
  18.4 0.2 pad_maximum_fusion
  18.6 2.9 %copy.44 = f32[3,3,256,256]{2,1,0,3:T(4,128)} copy(f32[3,3,256,256]{3,2,1,0:T(8,128)S(1)} %pad_maximum_fusion) | data formatting | bytes 4718592 | tf_op jit(solution)/shard_map/stack | solution.py:49
  21.5 0.6 copy-done.6
  22.2 0.6 dynamic-slice
  23.4 69.3 %all-reduce.4.cloned.1.call-done = f32[3,3,256,256]{2,1,0,3:T(4,128)} async-done(((f32[3,3,256,256]{2,1,0,3:T(4,128)}), f32[3,3,256,256]{2,1,0,3:T(4,128)}) %all-reduce.4.cloned.1.call-update) | async-done | bytes 2359312
  92.7 1.3 constant_dynamic-slice_fusion
  94.0 0.1 copy.46
  94.1 1.5 collective-permute-start.4
  95.7 13.5 %collective-permute-done.4 = f32[3,3,256,64]{2,3,1,0:T(8,128)S(1)} collective-permute-done((f32[3,3,256,64]{2,3,1,0:T(8,128)S(1)}, f32[3,3,256,64]{2,3,1,0:T(8,128)S(1)}, u32[]{:S(2)}, u32[]{:S(2)}) %collective-permute-start.4) | collective-permute-done | bytes 589856 | tf_op jit(solution)/shard_map/ppermute | solution.py:54
  109.1 0.1 copy_add_fusion
  109.3 1.6 collective-permute-start.5
  110.8 1.3 collective-permute-start.2
  112.1 1.3 collective-permute-start.3
  113.5 0.3 copy.49
  113.7 0.1 pad.5.clone
  113.8 0.2 copy.38
  114.0 0.4 copy-done.7
  114.4 1.2 fusion
  115.6 0.1 copy.39
  115.8 7.6 %collective-permute-done.5 = f32[3,3,256,64]{2,3,1,0:T(8,128)S(1)} collective-permute-done((f32[3,3,256,64]{2,3,1,0:T(8,128)S(1)}, f32[3,3,256,64]{2,3,1,0:T(8,128)S(1)}, u32[]{:S(2)}, u32[]{:S(2)}) %collective-permute-start.5) | collective-permute-done | bytes 589856 | tf_op jit(solution)/shard_map/ppermute | solution.py:54
  123.4 0.1 add.14
  123.5 2.5 %collective-permute-start.6 = (f32[3,3,256,64]{2,3,1,0:T(8,128)S(1)}, f32[3,3,256,64]{2,3,1,0:T(8,128)S(1)}, u32[]{:S(2)}, u32[]{:S(2)}) collective-permute-start(f32[3,3,256,64]{2,3,1,0:T(8,128)S(1)} %add.14), channel_id=1, source_target_pairs={{0,16},{4,20},{8,24},{12,28},{16,0},{20,4},{24,8},{28,12},{1,17},{... | collective-permute-start | bytes 1769480 | tf_op jit(solution)/shard_map/ppermute | solution.py:54
  126.0 0.1 maximum_bitcast_fusion.3
  126.0 0.9 copy.47
  126.9 0.3 copy.50
  127.2 0.1 pad.7.clone
  127.2 0.2 copy.42
  127.4 1.2 fusion.1
  128.7 0.1 copy.43
  128.8 0.9 copy.48
  129.7 20.5 %collective-permute-done.6 = f32[3,3,256,64]{2,3,1,0:T(8,128)S(1)} collective-permute-done((f32[3,3,256,64]{2,3,1,0:T(8,128)S(1)}, f32[3,3,256,64]{2,3,1,0:T(8,128)S(1)}, u32[]{:S(2)}, u32[]{:S(2)}) %collective-permute-start.6) | collective-permute-done | bytes 589856 | tf_op jit(solution)/shard_map/ppermute | solution.py:54
  150.2 0.9 add_multiply_fusion
  (26 shorter events, 0.2 us)
Async XLA Ops:
  7.2 106.8 %copy-start = (bf16[3,3,256,256]{3,2,1,0:T(8,128)(2,1)S(1)}, bf16[3,3,256,256]{3,2,1,0:T(8,128)(2,1)}, u32[]{:S(2)}) copy-start(bf16[3,3,256,256]{3,2,1,0:T(8,128)(2,1)} %param.4) | copy-start | bytes 3538948
  7.2 6.1 %copy-start.3 = (bf16[1,12,64,256]{3,2,1,0:T(8,128)(2,1)S(1)}, bf16[1,12,64,256]{3,2,1,0:T(8,128)(2,1)}, u32[]{:S(2)}) copy-start(bf16[1,12,64,256]{3,2,1,0:T(8,128)(2,1)} %param.3) | copy-start | bytes 1179652
  7.2 8.5 %copy-start.1 = (bf16[1,12,64,256]{3,2,1,0:T(8,128)(2,1)S(1)}, bf16[1,12,64,256]{3,2,1,0:T(8,128)(2,1)}, u32[]{:S(2)}) copy-start(bf16[1,12,64,256]{3,2,1,0:T(8,128)(2,1)} %param.5) | copy-start | bytes 1179652
  7.2 85.5 %all-reduce.4.cloned.1.call-start = ((), (), s32[]{:S(2)}) async-start(), calls=%async_computation | async-start | bytes 6291456
  8.2 5.1 %collective-permute-start = (bf16[1,1,64,256]{3,2,1,0:T(8,128)(2,1)S(1)}, bf16[1,1,64,256]{3,2,1,0:T(8,128)(2,1)S(1)}, u32[]{:S(2)}, u32[]{:S(2)}) collective-permute-start(bf16[1,1,64,256]{3,2,1,0:T(8,128)(2,1)S(1)} %get-tuple-element.18), channel_id=1, source_target_pairs={{0,1},{1,2},{2,3},{4,5},{5,6},{6,7},{8,9},{9,10},{10,11},{12,13},{... | collective-permute-start | bytes 98312 | tf_op jit(solution)/shard_map/ppermute | solution.py:14
  10.5 5.2 %collective-permute-start.1 = (bf16[1,1,64,256]{3,2,1,0:T(8,128)(2,1)S(1)}, bf16[1,1,64,256]{3,2,1,0:T(8,128)(2,1)S(1)}, u32[]{:S(2)}, u32[]{:S(2)}) collective-permute-start(bf16[1,1,64,256]{3,2,1,0:T(8,128)(2,1)S(1)} %get-tuple-element.17), channel_id=1, source_target_pairs={{1,0},{2,1},{3,2},{5,4},{6,5},{7,6},{9,8},{10,9},{11,10},{13,12},{... | collective-permute-start | bytes 98312 | tf_op jit(solution)/shard_map/ppermute | solution.py:15
  15.7 1.6 copy-start.4
  21.5 0.7 copy-start.6
  94.1 16.7 %copy-start.2 = (bf16[1,12,64,256]{3,2,1,0:T(8,128)(2,1)S(1)}, bf16[1,12,64,256]{3,2,1,0:T(8,128)(2,1)}, u32[]{:S(2)}) copy-start(bf16[1,12,64,256]{3,2,1,0:T(8,128)(2,1)} %param.5) | copy-start | bytes 1179652
  94.1 19.3 %copy-start.5 = (bf16[1,14,64,256]{3,2,1,0:T(8,128)(2,1)S(1)}, bf16[1,14,64,256]{3,2,1,0:T(8,128)(2,1)}, u32[]{:S(2)}) copy-start(bf16[1,14,64,256]{3,2,1,0:T(8,128)(2,1)} %copy-done.4) | copy-start | bytes 1376260
  94.1 15.0 %collective-permute-start.4 = (f32[3,3,256,64]{2,3,1,0:T(8,128)S(1)}, f32[3,3,256,64]{2,3,1,0:T(8,128)S(1)}, u32[]{:S(2)}, u32[]{:S(2)}) collective-permute-start(f32[3,3,256,64]{2,3,1,0:T(8,128)S(1)} %copy.46), channel_id=1, source_target_pairs={{0,4},{4,0},{8,12},{12,8},{16,20},{20,16},{24,28},{28,24},{1,5},{5... | collective-permute-start | bytes 1769480 | tf_op jit(solution)/shard_map/ppermute | solution.py:54
  109.3 14.1 %collective-permute-start.5 = (f32[3,3,256,64]{2,3,1,0:T(8,128)S(1)}, f32[3,3,256,64]{2,3,1,0:T(8,128)S(1)}, u32[]{:S(2)}, u32[]{:S(2)}) collective-permute-start(f32[3,3,256,64]{2,3,1,0:T(8,128)S(1)} %copy_add_fusion), channel_id=1, source_target_pairs={{0,8},{4,12},{8,0},{12,4},{16,24},{20,28},{24,16},{28,20},{1,9},{5... | collective-permute-start | bytes 1769480 | tf_op jit(solution)/shard_map/ppermute | solution.py:54
  110.8 15.1 %collective-permute-start.2 = (bf16[1,1,64,256]{3,2,1,0:T(8,128)(2,1)S(1)}, bf16[1,1,64,256]{3,2,1,0:T(8,128)(2,1)S(1)}, u32[]{:S(2)}, u32[]{:S(2)}) collective-permute-start(bf16[1,1,64,256]{3,2,1,0:T(8,128)(2,1)S(1)} %get-tuple-element.15), channel_id=1, source_target_pairs={{0,1},{1,2},{2,3},{4,5},{5,6},{6,7},{8,9},{9,10},{10,11},{12,13},{... | collective-permute-start | bytes 98312 | tf_op jit(solution)/shard_map/ppermute | solution.py:14
  112.1 13.8 %collective-permute-start.3 = (bf16[1,1,64,256]{3,2,1,0:T(8,128)(2,1)S(1)}, bf16[1,1,64,256]{3,2,1,0:T(8,128)(2,1)S(1)}, u32[]{:S(2)}, u32[]{:S(2)}) collective-permute-start(bf16[1,1,64,256]{3,2,1,0:T(8,128)(2,1)S(1)} %get-tuple-element.16), channel_id=1, source_target_pairs={{1,0},{2,1},{3,2},{5,4},{6,5},{7,6},{9,8},{10,9},{11,10},{13,12},{... | collective-permute-start | bytes 98312 | tf_op jit(solution)/shard_map/ppermute | solution.py:15
  113.7 0.7 copy-start.7
  123.5 26.7 %collective-permute-start.6 = (f32[3,3,256,64]{2,3,1,0:T(8,128)S(1)}, f32[3,3,256,64]{2,3,1,0:T(8,128)S(1)}, u32[]{:S(2)}, u32[]{:S(2)}) collective-permute-start(f32[3,3,256,64]{2,3,1,0:T(8,128)S(1)} %add.14), channel_id=1, source_target_pairs={{0,16},{4,20},{8,24},{12,28},{16,0},{20,4},{24,8},{28,12},{1,17},{... | collective-permute-start | bytes 1769480 | tf_op jit(solution)/shard_map/ppermute | solution.py:54
Sparse Core Ops, SparseCore 0:
  21.6 71.0 all-reduce.3
